TPU v7x, 512 devices: a whole 4x8x8 slice. The times are simulated.
512 devices in a mesh: group: 16 (over x_lo, z), tile: 32 (over x_hi, y, core).
Axes of the slice: x: 4 (x_hi: 2, x_lo: 2; x = x_hi * 2 + x_lo), y: 8, z: 8, core: 2. Of those that a mesh axis runs over, the one named last changes fastest.
Arguments:
- initial_state: float32 [48, 2, 128, 384], P(None, None, 'tile'), may hold values from -3 to 3
- perturbation: float32 [16, 48, 2, 128, 384], P('group', None, None, 'tile'), may hold values from -16 to 16
- land_sea: int32 [128, 384], P('tile'), may hold values 0 or 1
- relax_level: int32 [128, 384], P('tile'), may hold values from 0 to 3
- vertical_mix: float32 [48], replicated, may hold values from 0.1 to 2
Outputs:
- adjoint_field: float32 [16, 48, 2, 128, 384], P('group', None, None, 'tile')
- gram: float32 [16, 16], P('group')
All inputs are finite; a program needn't handle non-finite values. No bound on the sum of `land_sea` on one device may be relied on, other than what follows from the above.
Results may differ from a plain program's by a relative error of at most 0.00024.
Values sent between devices are 32-bit elements; how exact they have to be, the bound alone decides.
No kernel may reach another device: no remote copies, remote signals or barrier semaphores. Data moves between devices by JAX's collectives and lax.ppermute only.
A program may use at most 64 MiB of HBM per device.

v0:
```python
import jax
import jax.numpy as jnp
from jax import lax
from jax.sharding import PartitionSpec as P

STEPS = 3
advection = 0.2
diffusion = 0.1
drag_rate = 0.3
relaxation = 0.125


def padded_2(cells, sides, width):
    for axis, dim in sides:
        count = lax.axis_size(axis)
        ends = count - 1
        head = lax.slice_in_dim(cells, 0, width, axis=dim)
        tail = lax.slice_in_dim(cells, cells.shape[dim] - width, cells.shape[dim], axis=dim)
        cells = jnp.concatenate(
            [
                lax.ppermute(tail, axis, [(i, (i + 1) % count) for i in range(ends)]),
                cells,
                lax.ppermute(head, axis, [((i + 1) % count, i) for i in range(ends)]),
            ],
            axis=dim,
        )
    return cells


def row_slope(padded):
    return 0.5 * (padded[:, :, 2:] - padded[:, :, :-2])


def laplace(padded, left, right):
    centre = padded[:, :, 1:-1]
    widened = jnp.concatenate([left, centre, right], axis=3)
    return (
        padded[:, :, 2:] + padded[:, :, :-2] + widened[..., 2:] + widened[..., :-2] - 4.0 * centre
    )


def mixing_inverse(mixing):
    nothing = jnp.zeros((1,), jnp.float32)
    upper_band = jnp.concatenate([-mixing[:-1], nothing])
    lower_band = jnp.concatenate([nothing, -mixing[:-1]])
    diagonal_band = 1.0 + mixing + jnp.concatenate([nothing, mixing[:-1]])
    identity = jnp.eye(mixing.shape[0], dtype=jnp.float32)
    return lax.linalg.tridiagonal_solve(lower_band, diagonal_band, upper_band, identity)


def column_solve(columns, inverse_mix):
    layout = columns.shape
    solved = jnp.dot(
        inverse_mix,
        columns.reshape(layout[0], -1),
        precision=lax.Precision.HIGHEST,
        preferred_element_type=jnp.float32,
    )
    return solved.reshape(layout)


def flat_rims(padded):
    blank = jnp.zeros(padded.shape[:2] + (padded.shape[2] - 2, 1), jnp.float32)
    return (padded, blank, blank)


def state_halo(field):
    return flat_rims(padded_2(field, (("tile", 2),), 1))


def tangent_halo(field):
    return flat_rims(padded_2(field, (("tile", 2),), 1))


def adjoint_halo(field):
    return flat_rims(padded_2(field, (("tile", 2),), 1))


def adjoint_step(adjoint, zonal_wind, slopes, landmask, nudging, inverse_mix, edges):
    backed = column_solve(adjoint, inverse_mix) * nudging
    back_u = backed[:, 0:1]
    back_t = backed[:, 1:2]
    stacked = jnp.concatenate([backed, zonal_wind * backed], axis=1)
    padded, left, right = edges(stacked)
    carried = row_slope(padded[:, 2:])
    spread = laplace(padded[:, :2], left[:, :2], right[:, :2])
    adj_u = (
        back_u
        - advection * back_u * slopes[:, 0:1]
        + advection * carried[:, 0:1]
        + diffusion * spread[:, 0:1]
        - drag_rate * landmask * back_u
        - advection * back_t * slopes[:, 1:2]
    )
    adj_t = back_t + advection * carried[:, 1:2] + diffusion * spread[:, 1:2]
    return jnp.concatenate([adj_u, adj_t], axis=1)


def per_device(initial_state, perturbation, land_sea, relax_level, vertical_mix):
    landmask = land_sea.astype(jnp.float32)
    nudging = 1.0 - relaxation * relax_level.astype(jnp.float32)
    select = (jnp.arange(2) == 0).astype(jnp.float32)[None, :, None, None]
    inverse_mix = mixing_inverse(vertical_mix)
    current = initial_state
    tangent = perturbation[0]
    history = []
    for position in range(STEPS):
        state_pad, state_left, state_right = state_halo(current)
        tangent_pad, tangent_left, tangent_right = tangent_halo(tangent)
        slopes = row_slope(state_pad)
        zonal_wind = current[:, 0:1]
        history.append((zonal_wind, slopes))
        if position + 1 < STEPS:
            updated = (
                current
                - advection * zonal_wind * slopes
                + diffusion * laplace(state_pad, state_left, state_right)
                - drag_rate * landmask * select * current
            )
            current = column_solve(updated * nudging, inverse_mix)
        changed = (
            tangent
            - advection * (tangent[:, 0:1] * slopes + zonal_wind * row_slope(tangent_pad))
            + diffusion * laplace(tangent_pad, tangent_left, tangent_right)
            - drag_rate * landmask * select * tangent
        )
        tangent = column_solve(changed * nudging, inverse_mix)
    adjoint = tangent
    for position in reversed(range(STEPS)):
        zonal_wind, slopes = history[position]
        adjoint = adjoint_step(
            adjoint, zonal_wind, slopes, landmask, nudging, inverse_mix, adjoint_halo
        )
    adjoint_field = adjoint[None]
    cell_count = adjoint.size * lax.axis_size("tile")
    values = lax.map(
        lambda member_row: jnp.sum(member_row * adjoint),
        lax.all_gather(adjoint_field, "group", axis=0, tiled=True),
    )
    whole_row = lax.psum(values, "tile")
    gram = whole_row[None] / cell_count
    return (adjoint_field, gram)


def solution(mesh):
    placed = (
        P(None, None, "tile", None),
        P("group", None, None, "tile", None),
        P("tile", None),
        P("tile", None),
        P(),
    )
    return jax.shard_map(
        per_device,
        mesh=mesh,
        in_specs=placed,
        out_specs=(P("group", None, None, "tile", None), P("group", None)),
        check_vma=False,
    )
```

profile of v0, /device:TPU:2, one launch (start us, length us, event | category | flops | bytes accessed | tf_op | source)
XLA Modules:
  0.0 532.5 jit_solution(14028871688670945358)
XLA Ops:
  7.2 1.2 copy.23
  8.4 1.3 collective-permute-start
  9.7 3.0 collective-permute-start.1
  12.8 1.2 copy.75
  14.0 1.3 collective-permute-start.2
  15.3 3.7 collective-permute-start.3
  114.5 30.1 %fusion.146 = (f32[1,48]{1,0:T(1,128)S(1)}, f32[48]{0:T(128)S(1)}, f32[48]{0:T(128)S(1)}, f32[48]{0:T(128)S(1)}, f32[48]{0:T(128)S(1)}, /*index=5*/f32[48]{0:T(1...) fusion(f32[]{:T(128)S(6)} %div.4795, ...), kind=kLoop, calls=%fused_computation.376 | loop fusion | flops 6912 | bytes 11904 | tf_op jit(solution)/shard_map/while/body/broadcast_in_dim | solution.py:48
  144.6 22.5 %subtract_divide_fusion = (f32[1,48]{1,0:T(1,128)S(1)}, f32[1,48]{1,0:T(1,128)S(1)}, f32[1,48]{1,0:T(1,128)S(1)}, f32[1,48]{1,0:T(1,128)S(1)}, f32[1,48]{1,0:T(1...) fusion(f32[48,48]{1,0:T(8,128)S(1)} %fusion.97, ...), kind=kLoop, calls=%fused_computation.339 | loop fusion | flops 5184 | bytes 14304 | tf_op jit(solution)/shard_map/eval_jaxpr/div | solution.py:48
  169.0 4.8 multiply_subtract_fusion.4
  173.8 2.2 concatenate.166
  180.2 1.4 fusion.15
  184.0 1.3 collective-permute-start.6
  185.2 4.3 collective-permute-start.7
  189.5 1.3 collective-permute-start.4
  190.8 4.3 collective-permute-start.5
  196.1 1.5 fusion.66
  200.5 1.4 fusion.29
  203.5 1.3 collective-permute-start.10
  204.8 5.4 %collective-permute-start.11 = (f32[48,2,1,384]{3,0,2,1:T(8,128)}, f32[48,2,1,384]{3,0,2,1:T(8,128)S(1)}, u32[]{:S(2)}, u32[]{:S(2)}) collective-permute-start(f32[48,2,1,384]{3,0,2,1:T(8,128)} %get-tuple-element.214), channel_id=1, source_target_pairs={{0,1},{1,2},{2,3},{3,4},{4,5},{5,6},{6,7},{7,8},{8,9},{9,10},{10,1... | collective-permute-start | bytes 442376 | tf_op jit(solution)/shard_map/ppermute | solution.py:21
  210.2 1.5 collective-permute-start.8
  211.6 5.0 collective-permute-start.9
  217.6 1.5 broadcast_multiply_fusion.3
  222.4 1.3 collective-permute-start.12
  223.7 5.4 %collective-permute-start.13 = (f32[48,4,1,384]{3,0,2,1:T(8,128)S(1)}, f32[48,4,1,384]{3,0,2,1:T(8,128)S(1)}, u32[]{:S(2)}, u32[]{:S(2)}) collective-permute-start(f32[48,4,1,384]{3,0,2,1:T(8,128)S(1)} %get-tuple-element.199), channel_id=1, source_target_pairs={{0,1},{1,2},{2,3},{3,4},{4,5},{5,6},{6,7},{7,8},{8,9},{9,10},{10,1... | collective-permute-start | bytes 884744 | tf_op jit(solution)/shard_map/ppermute | solution.py:21
  232.4 1.3 collective-permute-start.14
  233.7 7.5 %collective-permute-start.15 = (f32[48,4,1,384]{3,0,2,1:T(8,128)S(1)}, f32[48,4,1,384]{3,0,2,1:T(8,128)S(1)}, u32[]{:S(2)}, u32[]{:S(2)}) collective-permute-start(f32[48,4,1,384]{3,0,2,1:T(8,128)S(1)} %get-tuple-element.197), channel_id=1, source_target_pairs={{0,1},{1,2},{2,3},{3,4},{4,5},{5,6},{6,7},{7,8},{8,9},{9,10},{10,1... | collective-permute-start | bytes 884744 | tf_op jit(solution)/shard_map/ppermute | solution.py:21
  244.5 1.3 collective-permute-start.16
  245.8 7.5 %collective-permute-start.17 = (f32[48,4,1,384]{3,0,2,1:T(8,128)S(1)}, f32[48,4,1,384]{3,0,2,1:T(8,128)S(1)}, u32[]{:S(2)}, u32[]{:S(2)}) collective-permute-start(f32[48,4,1,384]{3,0,2,1:T(8,128)S(1)} %get-tuple-element.195), channel_id=1, source_target_pairs={{0,1},{1,2},{2,3},{3,4},{4,5},{5,6},{6,7},{7,8},{8,9},{9,10},{10,1... | collective-permute-start | bytes 884744 | tf_op jit(solution)/shard_map/ppermute | solution.py:21
  256.0 1.3 copy.47
  258.3 152.9 %all-gather.3.cloned.1.call-done = f32[768,2,4,384]{3,0,2,1:T(8,128)} async-done(((f32[48,2,4,384]{3,0,2,1:T(8,128)}), f32[768,2,4,384]{3,0,2,1:T(8,128)}) %all-gather.3.cloned.1.call-update) | async-done | bytes 9437200 | tf_op jit(solution)/shard_map/all_gather | solution.py:138
  411.3 44.8 %while.2 = (s32[]{:T(128)}, f32[16]{0:T(128)S(1)}, f32[16,48,2,4,384]{4,1,0,3,2:T(8,128)}, f32[48,2,4,384]{3,2,1,0:T(4,128)S(1)}, s32[]{:T(128)}) while((s32[]{:T(128)}, f32[16]{0:T(128)S(1)}, f32[16,48,2,4,384]{4,1,0,3,2:T(8,128)}, f32[48,2,4,384]{3,2,1,0:T(4,128)S(1)}, s32[]{:T(128)}) %tuple.238), condition=%wide.region_2.3_spmd, body=%wide.region_0.2_spmd.sunk | while | flops 294913 | bytes 2359377 | solution.py:136
  456.1 69.1 %psum.7 = f32[16]{0:T(128)S(1)} all-reduce(f32[16]{0:T(128)S(1)} %get-tuple-element.58), channel_id=1, replica_groups=mesh['group'=16,'tile'=32] {'tile'}, use_global_device_ids=true, to_apply=%region_3.4 | all-reduce | flops 16 | bytes 128 | tf_op jit(solution)/shard_map/psum | solution.py:140
  (150 shorter events, 79.8 us)
Async XLA Ops:
  7.2 404.1 %all-gather.3.cloned.1.call-start = ((), (), s32[]{:S(2)}) async-start(), calls=%async_computation | async-start | bytes 10027008 | tf_op jit(solution)/shard_map/all_gather | solution.py:138
  8.4 168.3 %collective-permute-start = (f32[48,2,1,384]{3,0,2,1:T(8,128)S(1)}, f32[48,2,1,384]{3,0,2,1:T(8,128)S(1)}, u32[]{:S(2)}, u32[]{:S(2)}) collective-permute-start(f32[48,2,1,384]{3,0,2,1:T(8,128)S(1)} %get-tuple-element.223), channel_id=1, source_target_pairs={{1,0},{2,1},{3,2},{4,3},{5,4},{6,5},{7,6},{8,7},{9,8},{10,9},{11,1... | collective-permute-start | bytes 442376 | tf_op jit(solution)/shard_map/ppermute | solution.py:23
  9.7 167.0 %collective-permute-start.1 = (f32[48,2,1,384]{3,0,2,1:T(8,128)S(1)}, f32[48,2,1,384]{3,0,2,1:T(8,128)S(1)}, u32[]{:S(2)}, u32[]{:S(2)}) collective-permute-start(f32[48,2,1,384]{3,0,2,1:T(8,128)S(1)} %get-tuple-element.222), channel_id=1, source_target_pairs={{0,1},{1,2},{2,3},{3,4},{4,5},{5,6},{6,7},{7,8},{8,9},{9,10},{10,1... | collective-permute-start | bytes 442376 | tf_op jit(solution)/shard_map/ppermute | solution.py:21
  14.0 162.7 %collective-permute-start.2 = (f32[48,2,1,384]{3,0,2,1:T(8,128)S(1)}, f32[48,2,1,384]{3,0,2,1:T(8,128)S(1)}, u32[]{:S(2)}, u32[]{:S(2)}) collective-permute-start(f32[48,2,1,384]{3,0,2,1:T(8,128)S(1)} %get-tuple-element.219), channel_id=1, source_target_pairs={{1,0},{2,1},{3,2},{4,3},{5,4},{6,5},{7,6},{8,7},{9,8},{10,9},{11,1... | collective-permute-start | bytes 442376 | tf_op jit(solution)/shard_map/ppermute | solution.py:23
  15.3 161.4 %collective-permute-start.3 = (f32[48,2,1,384]{3,0,2,1:T(8,128)S(1)}, f32[48,2,1,384]{3,0,2,1:T(8,128)S(1)}, u32[]{:S(2)}, u32[]{:S(2)}) collective-permute-start(f32[48,2,1,384]{3,0,2,1:T(8,128)S(1)} %get-tuple-element.218), channel_id=1, source_target_pairs={{0,1},{1,2},{2,3},{3,4},{4,5},{5,6},{6,7},{7,8},{8,9},{9,10},{10,1... | collective-permute-start | bytes 442376 | tf_op jit(solution)/shard_map/ppermute | solution.py:21
  176.7 1.0 copy-start.1
  184.0 11.2 %collective-permute-start.6 = (f32[48,2,1,384]{3,0,2,1:T(8,128)}, f32[48,2,1,384]{3,0,2,1:T(8,128)S(1)}, u32[]{:S(2)}, u32[]{:S(2)}) collective-permute-start(f32[48,2,1,384]{3,0,2,1:T(8,128)} %get-tuple-element.217), channel_id=1, source_target_pairs={{1,0},{2,1},{3,2},{4,3},{5,4},{6,5},{7,6},{8,7},{9,8},{10,9},{11,1... | collective-permute-start | bytes 442376 | tf_op jit(solution)/shard_map/ppermute | solution.py:23
  185.2 9.9 %collective-permute-start.7 = (f32[48,2,1,384]{3,0,2,1:T(8,128)}, f32[48,2,1,384]{3,0,2,1:T(8,128)S(1)}, u32[]{:S(2)}, u32[]{:S(2)}) collective-permute-start(f32[48,2,1,384]{3,0,2,1:T(8,128)} %get-tuple-element.216), channel_id=1, source_target_pairs={{0,1},{1,2},{2,3},{3,4},{4,5},{5,6},{6,7},{7,8},{8,9},{9,10},{10,1... | collective-permute-start | bytes 442376 | tf_op jit(solution)/shard_map/ppermute | solution.py:21
  189.5 5.6 %collective-permute-start.4 = (f32[48,2,1,384]{3,0,2,1:T(8,128)S(1)}, f32[48,2,1,384]{3,0,2,1:T(8,128)S(1)}, u32[]{:S(2)}, u32[]{:S(2)}) collective-permute-start(f32[48,2,1,384]{3,0,2,1:T(8,128)S(1)} %get-tuple-element.221), channel_id=1, source_target_pairs={{1,0},{2,1},{3,2},{4,3},{5,4},{6,5},{7,6},{8,7},{9,8},{10,9},{11,1... | collective-permute-start | bytes 442376 | tf_op jit(solution)/shard_map/ppermute | solution.py:23
  190.8 5.3 collective-permute-start.5
  196.1 1.5 copy-start.2
  203.5 13.9 %collective-permute-start.10 = (f32[48,2,1,384]{3,0,2,1:T(8,128)}, f32[48,2,1,384]{3,0,2,1:T(8,128)S(1)}, u32[]{:S(2)}, u32[]{:S(2)}) collective-permute-start(f32[48,2,1,384]{3,0,2,1:T(8,128)} %get-tuple-element.215), channel_id=1, source_target_pairs={{1,0},{2,1},{3,2},{4,3},{5,4},{6,5},{7,6},{8,7},{9,8},{10,9},{11,1... | collective-permute-start | bytes 442376 | tf_op jit(solution)/shard_map/ppermute | solution.py:23
  204.8 12.6 %collective-permute-start.11 = (f32[48,2,1,384]{3,0,2,1:T(8,128)}, f32[48,2,1,384]{3,0,2,1:T(8,128)S(1)}, u32[]{:S(2)}, u32[]{:S(2)}) collective-permute-start(f32[48,2,1,384]{3,0,2,1:T(8,128)} %get-tuple-element.214), channel_id=1, source_target_pairs={{0,1},{1,2},{2,3},{3,4},{4,5},{5,6},{6,7},{7,8},{8,9},{9,10},{10,1... | collective-permute-start | bytes 442376 | tf_op jit(solution)/shard_map/ppermute | solution.py:21
  210.2 7.2 %collective-permute-start.8 = (f32[48,2,1,384]{3,0,2,1:T(8,128)S(1)}, f32[48,2,1,384]{3,0,2,1:T(8,128)S(1)}, u32[]{:S(2)}, u32[]{:S(2)}) collective-permute-start(f32[48,2,1,384]{3,0,2,1:T(8,128)S(1)} %get-tuple-element.212), channel_id=1, source_target_pairs={{1,0},{2,1},{3,2},{4,3},{5,4},{6,5},{7,6},{8,7},{9,8},{10,9},{11,1... | collective-permute-start | bytes 442376 | tf_op jit(solution)/shard_map/ppermute | solution.py:23
  211.6 6.0 %collective-permute-start.9 = (f32[48,2,1,384]{3,0,2,1:T(8,128)S(1)}, f32[48,2,1,384]{3,0,2,1:T(8,128)S(1)}, u32[]{:S(2)}, u32[]{:S(2)}) collective-permute-start(f32[48,2,1,384]{3,0,2,1:T(8,128)S(1)} %get-tuple-element.213), channel_id=1, source_target_pairs={{0,1},{1,2},{2,3},{3,4},{4,5},{5,6},{6,7},{7,8},{8,9},{9,10},{10,1... | collective-permute-start | bytes 442376 | tf_op jit(solution)/shard_map/ppermute | solution.py:21
  221.2 10.5 %copy-start = (f32[48,4,384]{2,0,1:T(8,128)S(1)}, f32[48,4,384]{2,0,1:T(8,128)}, u32[]{:S(2)}) copy-start(f32[48,4,384]{2,0,1:T(8,128)} %get-tuple-element.210) | copy-start | bytes 884740
  222.4 6.7 %collective-permute-start.12 = (f32[48,4,1,384]{3,0,2,1:T(8,128)S(1)}, f32[48,4,1,384]{3,0,2,1:T(8,128)S(1)}, u32[]{:S(2)}, u32[]{:S(2)}) collective-permute-start(f32[48,4,1,384]{3,0,2,1:T(8,128)S(1)} %get-tuple-element.198), channel_id=1, source_target_pairs={{1,0},{2,1},{3,2},{4,3},{5,4},{6,5},{7,6},{8,7},{9,8},{10,9},{11,1... | collective-permute-start | bytes 884744 | tf_op jit(solution)/shard_map/ppermute | solution.py:23
  223.7 6.6 %collective-permute-start.13 = (f32[48,4,1,384]{3,0,2,1:T(8,128)S(1)}, f32[48,4,1,384]{3,0,2,1:T(8,128)S(1)}, u32[]{:S(2)}, u32[]{:S(2)}) collective-permute-start(f32[48,4,1,384]{3,0,2,1:T(8,128)S(1)} %get-tuple-element.199), channel_id=1, source_target_pairs={{0,1},{1,2},{2,3},{3,4},{4,5},{5,6},{6,7},{7,8},{8,9},{9,10},{10,1... | collective-permute-start | bytes 884744 | tf_op jit(solution)/shard_map/ppermute | solution.py:21
  232.4 8.8 %collective-permute-start.14 = (f32[48,4,1,384]{3,0,2,1:T(8,128)S(1)}, f32[48,4,1,384]{3,0,2,1:T(8,128)S(1)}, u32[]{:S(2)}, u32[]{:S(2)}) collective-permute-start(f32[48,4,1,384]{3,0,2,1:T(8,128)S(1)} %get-tuple-element.196), channel_id=1, source_target_pairs={{1,0},{2,1},{3,2},{4,3},{5,4},{6,5},{7,6},{8,7},{9,8},{10,9},{11,1... | collective-permute-start | bytes 884744 | tf_op jit(solution)/shard_map/ppermute | solution.py:23
  233.7 8.7 %collective-permute-start.15 = (f32[48,4,1,384]{3,0,2,1:T(8,128)S(1)}, f32[48,4,1,384]{3,0,2,1:T(8,128)S(1)}, u32[]{:S(2)}, u32[]{:S(2)}) collective-permute-start(f32[48,4,1,384]{3,0,2,1:T(8,128)S(1)} %get-tuple-element.197), channel_id=1, source_target_pairs={{0,1},{1,2},{2,3},{3,4},{4,5},{5,6},{6,7},{7,8},{8,9},{9,10},{10,1... | collective-permute-start | bytes 884744 | tf_op jit(solution)/shard_map/ppermute | solution.py:21
  244.5 8.8 %collective-permute-start.16 = (f32[48,4,1,384]{3,0,2,1:T(8,128)S(1)}, f32[48,4,1,384]{3,0,2,1:T(8,128)S(1)}, u32[]{:S(2)}, u32[]{:S(2)}) collective-permute-start(f32[48,4,1,384]{3,0,2,1:T(8,128)S(1)} %get-tuple-element.194), channel_id=1, source_target_pairs={{1,0},{2,1},{3,2},{4,3},{5,4},{6,5},{7,6},{8,7},{9,8},{10,9},{11,1... | collective-permute-start | bytes 884744 | tf_op jit(solution)/shard_map/ppermute | solution.py:23
  245.8 8.7 %collective-permute-start.17 = (f32[48,4,1,384]{3,0,2,1:T(8,128)S(1)}, f32[48,4,1,384]{3,0,2,1:T(8,128)S(1)}, u32[]{:S(2)}, u32[]{:S(2)}) collective-permute-start(f32[48,4,1,384]{3,0,2,1:T(8,128)S(1)} %get-tuple-element.195), channel_id=1, source_target_pairs={{0,1},{1,2},{2,3},{3,4},{4,5},{5,6},{6,7},{7,8},{8,9},{9,10},{10,1... | collective-permute-start | bytes 884744 | tf_op jit(solution)/shard_map/ppermute | solution.py:21
Sparse Core Ops, SparseCore 0:
  256.1 155.1 all-gather.2
where the time goes:
time: 536 us; the launch traced here: 533 us
  waiting for transfers between devices  158 us (29%)
  between operations  104 us (19%)
  other arithmetic  90.6 us (17%)
  blocking collectives  69.1 us (13%)
  starting transfers between devices  57.9 us (11%)
  local copies, waits for them, and re-layouts  48.3 us (9%)
    all_gather x1, waiting for transfers between devices, per_device(): lax.all_gather(adjoint_field, 'group', axis=0, tiled=True)  153 us
    psum x1, blocking collectives, per_device(): whole_row = lax.psum(values, 'tile')  69.1 us
    ppermute x9, starting transfers between devices, padded_2(): lax.ppermute(tail, axis, [(i, (i + 1) % count) for i in range(ends)])  46 us
    broadcast_in_dim x3, other arithmetic, mixing_inverse(): lax.linalg.tridiagonal_solve(lower_band, diagonal_band, upper_band, ident...  31.2 us
    div x1, other arithmetic, mixing_inverse(): lax.linalg.tridiagonal_solve(lower_band, diagonal_band, upper_band, ident...  22.5 us
    dynamic_slice x16, local copies, waits for them, and re-layouts, per_device(): lax.map(lambda member_row: jnp.sum(member_row * adjoint), lax.all_gather(...  17.7 us
    reduce_sum x16, other arithmetic, per_device(): jnp.sum(member_row * adjoint)  15.2 us
    dynamic_update_slice x16, local copies, waits for them, and re-layouts, per_device(): lax.map(lambda member_row: jnp.sum(member_row * adjoint), lax.all_gather(...  11.9 us
  transfers between devices with their start and end apart: 19, of which 6 were waited for; matrix products, arithmetic and copies ran while one was open for 14% of the time, Pallas kernels for 0%

commit v1 on v0

--- a/solution.py
+++ b/solution.py
@@ -135,7 +135,10 @@
     cell_count = adjoint.size * lax.axis_size("tile")
     values = lax.map(
         lambda member_row: jnp.sum(member_row * adjoint),
-        lax.all_gather(adjoint_field, "group", axis=0, tiled=True),
+        jnp.concatenate(
+            lax.all_to_all(jnp.stack([adjoint_field] * lax.axis_size("group")), "group", 0, 0),
+            axis=0,
+        ),
     )
     whole_row = lax.psum(values, "tile")
     gram = whole_row[None] / cell_count

time: 536 us -> 622 us (1.16)
  the two profiles are of different devices: /device:TPU:2 before, /device:TPU:135 now
where the time goes in v1:
time: 622 us; the launch traced here: 618 us
  waiting for transfers between devices  227 us (36%)
  other arithmetic  105 us (17%)
  between operations  90 us (14%)
  starting transfers between devices  89.4 us (14%)
  blocking collectives  67.1 us (11%)
  local copies, waits for them, and re-layouts  33.5 us (5%)
    all_to_all x1, waiting for transfers between devices, per_device(): lax.all_to_all(jnp.stack([adjoint_field] * lax.axis_size('group')), 'grou...  206 us
    psum x1, blocking collectives, per_device(): whole_row = lax.psum(values, 'tile')  67.1 us
    ppermute x9, starting transfers between devices, padded_2(): lax.ppermute(head, axis, [((i + 1) % count, i) for i in range(ends)])  61 us
    reduce_sum x16, other arithmetic, per_device(): jnp.sum(member_row * adjoint)  31.1 us
    broadcast_in_dim x3, other arithmetic, mixing_inverse(): lax.linalg.tridiagonal_solve(lower_band, diagonal_band, upper_band, ident...  31 us
    div x1, other arithmetic, mixing_inverse(): lax.linalg.tridiagonal_solve(lower_band, diagonal_band, upper_band, ident...  22.4 us
    ppermute x9, waiting for transfers between devices, padded_2(): lax.ppermute(tail, axis, [(i, (i + 1) % count) for i in range(ends)])  20.3 us
    ppermute x9, starting transfers between devices, padded_2(): lax.ppermute(tail, axis, [(i, (i + 1) % count) for i in range(ends)])  19.9 us
  transfers between devices with their start and end apart: 19, of which 7 were waited for; matrix products, arithmetic and copies ran while one was open for 12% of the time, Pallas kernels for 0%

profile of v1, /device:TPU:135, one launch (start us, length us, event | category | flops | bytes accessed | tf_op | source)
XLA Modules:
  0.0 617.6 jit_solution(1054496653768564576)
XLA Ops:
  1.8 2.6 collective-permute-start
  4.4 3.1 collective-permute-start.1
  8.8 4.5 collective-permute-start.2
  110.3 30.0 %fusion.145 = (f32[1,48]{1,0:T(1,128)S(1)}, f32[48]{0:T(128)S(1)}, f32[48]{0:T(128)S(1)}, f32[48]{0:T(128)S(1)}, f32[48]{0:T(128)S(1)}, /*index=5*/f32[48]{0:T(1...) fusion(f32[]{:T(128)S(6)} %div.4795, ...), kind=kLoop, calls=%fused_computation.374 | loop fusion | flops 6912 | bytes 11904 | tf_op jit(solution)/shard_map/while/body/broadcast_in_dim | solution.py:48
  140.3 22.4 %subtract_divide_fusion = (f32[1,48]{1,0:T(1,128)S(1)}, f32[1,48]{1,0:T(1,128)S(1)}, f32[1,48]{1,0:T(1,128)S(1)}, f32[1,48]{1,0:T(1,128)S(1)}, f32[1,48]{1,0:T(1...) fusion(f32[48,48]{1,0:T(8,128)S(1)} %fusion.96, ...), kind=kLoop, calls=%fused_computation.337 | loop fusion | flops 5184 | bytes 14304 | tf_op jit(solution)/shard_map/eval_jaxpr/div | solution.py:48
  164.5 4.7 multiply_subtract_fusion.4
  169.2 2.2 concatenate.166
  179.4 7.2 %collective-permute-start.6 = (f32[48,2,1,384]{3,0,2,1:T(8,128)}, f32[48,2,1,384]{3,0,2,1:T(8,128)S(1)}, u32[]{:S(2)}, u32[]{:S(2)}) collective-permute-start(f32[48,2,1,384]{3,0,2,1:T(8,128)} %get-tuple-element.223), channel_id=1, source_target_pairs={{1,0},{2,1},{3,2},{4,3},{5,4},{6,5},{7,6},{8,7},{9,8},{10,9},{11,1... | collective-permute-start | bytes 442376 | tf_op jit(solution)/shard_map/ppermute | solution.py:23
  188.5 7.3 %collective-permute-start.4 = (f32[48,2,1,384]{3,0,2,1:T(8,128)S(1)}, f32[48,2,1,384]{3,0,2,1:T(8,128)S(1)}, u32[]{:S(2)}, u32[]{:S(2)}) collective-permute-start(f32[48,2,1,384]{3,0,2,1:T(8,128)S(1)} %get-tuple-element.227), channel_id=1, source_target_pairs={{1,0},{2,1},{3,2},{4,3},{5,4},{6,5},{7,6},{8,7},{9,8},{10,9},{11,1... | collective-permute-start | bytes 442376 | tf_op jit(solution)/shard_map/ppermute | solution.py:23
  197.8 6.1 collective-permute-done.5
  211.3 9.2 %collective-permute-start.10 = (f32[48,2,1,384]{3,0,2,1:T(8,128)}, f32[48,2,1,384]{3,0,2,1:T(8,128)S(1)}, u32[]{:S(2)}, u32[]{:S(2)}) collective-permute-start(f32[48,2,1,384]{3,0,2,1:T(8,128)} %get-tuple-element.221), channel_id=1, source_target_pairs={{1,0},{2,1},{3,2},{4,3},{5,4},{6,5},{7,6},{8,7},{9,8},{10,9},{11,1... | collective-permute-start | bytes 442376 | tf_op jit(solution)/shard_map/ppermute | solution.py:23
  222.5 2.4 collective-permute-start.8
  224.9 3.3 collective-permute-start.9
  229.2 3.3 collective-permute-done.9
  237.3 9.2 %collective-permute-start.12 = (f32[48,4,1,384]{3,0,2,1:T(8,128)S(1)}, f32[48,4,1,384]{3,0,2,1:T(8,128)S(1)}, u32[]{:S(2)}, u32[]{:S(2)}) collective-permute-start(f32[48,4,1,384]{3,0,2,1:T(8,128)S(1)} %get-tuple-element.204), channel_id=1, source_target_pairs={{1,0},{2,1},{3,2},{4,3},{5,4},{6,5},{7,6},{8,7},{9,8},{10,9},{11,1... | collective-permute-start | bytes 884744 | tf_op jit(solution)/shard_map/ppermute | solution.py:23
  248.4 3.6 collective-permute-done.13
  254.2 8.0 %collective-permute-start.14 = (f32[48,4,1,384]{3,0,2,1:T(8,128)S(1)}, f32[48,4,1,384]{3,0,2,1:T(8,128)S(1)}, u32[]{:S(2)}, u32[]{:S(2)}) collective-permute-start(f32[48,4,1,384]{3,0,2,1:T(8,128)S(1)} %get-tuple-element.202), channel_id=1, source_target_pairs={{1,0},{2,1},{3,2},{4,3},{5,4},{6,5},{7,6},{8,7},{9,8},{10,9},{11,1... | collective-permute-start | bytes 884744 | tf_op jit(solution)/shard_map/ppermute | solution.py:23
  264.2 3.6 collective-permute-done.15
  269.9 10.6 %collective-permute-start.16 = (f32[48,4,1,384]{3,0,2,1:T(8,128)S(1)}, f32[48,4,1,384]{3,0,2,1:T(8,128)S(1)}, u32[]{:S(2)}, u32[]{:S(2)}) collective-permute-start(f32[48,4,1,384]{3,0,2,1:T(8,128)S(1)} %get-tuple-element.200), channel_id=1, source_target_pairs={{1,0},{2,1},{3,2},{4,3},{5,4},{6,5},{7,6},{8,7},{9,8},{10,9},{11,1... | collective-permute-start | bytes 884744 | tf_op jit(solution)/shard_map/ppermute | solution.py:23
  282.5 3.6 collective-permute-done.17
  287.1 5.5 stack.3
  292.6 8.4 %all-to-all-start = ((f32[16,1,48,2,4,384]{5,4,3,2,1,0:T(4,128)}), f32[16,1,48,2,4,384]{5,4,3,2,1,0:T(4,128)}, u32[]{:S(2)}, u32[]{:S(2)}) async-start(f32[16,1,48,2,4,384]{5,4,3,2,1,0:T(4,128)} %stack.3), calls=%async_computation | async-start | bytes 18874368 | tf_op jit(solution)/shard_map/all_to_all | solution.py:139
  302.0 206.4 %all-to-all-done = f32[16,1,48,2,4,384]{5,4,3,2,1,0:T(4,128)} async-done(((f32[16,1,48,2,4,384]{5,4,3,2,1,0:T(4,128)}), f32[16,1,48,2,4,384]{5,4,3,2,1,0:T(4,128)}, u32[]{:S(2)}, u32[]{:S(2)}) %all-to-all-start) | async-done | bytes 9437216 | tf_op jit(solution)/shard_map/all_to_all | solution.py:139
  508.4 41.6 %while.2 = (s32[]{:T(128)}, f32[16]{0:T(128)S(1)}, f32[16,48,2,4,384]{4,3,2,1,0:T(4,128)}, f32[48,2,4,384]{3,2,1,0:T(4,128)S(1)}, s32[]{:T(128)}) while((s32[]{:T(128)}, f32[16]{0:T(128)S(1)}, f32[16,48,2,4,384]{4,3,2,1,0:T(4,128)}, f32[48,2,4,384]{3,2,1,0:T(4,128)S(1)}, s32[]{:T(128)}) %tuple.235), condition=%wide.region_2.3_spmd, body=%wide.region_0.2_spmd.sunk | while | flops 294913 | bytes 1179729 | solution.py:136
  511.0 1.9 fusion.178
  513.6 1.9 fusion.178
  516.2 1.9 fusion.178
  518.8 1.9 fusion.178
  542.2 1.9 fusion.178
  544.8 1.9 fusion.178
  547.4 1.9 fusion.178
  550.0 67.1 %psum.7 = f32[16]{0:T(128)S(1)} all-reduce(f32[16]{0:T(128)S(1)} %get-tuple-element.58), channel_id=1, replica_groups=mesh['group'=16,'tile'=32] {'tile'}, use_global_device_ids=true, to_apply=%region_3.4 | all-reduce | flops 16 | bytes 128 | tf_op jit(solution)/shard_map/psum | solution.py:143
  (134 shorter events, 79.6 us)
Async XLA Ops:
  1.8 170.3 %collective-permute-start = (f32[48,2,1,384]{3,0,2,1:T(8,128)S(1)}, f32[48,2,1,384]{3,0,2,1:T(8,128)S(1)}, u32[]{:S(2)}, u32[]{:S(2)}) collective-permute-start(f32[48,2,1,384]{3,0,2,1:T(8,128)S(1)} %get-tuple-element.229), channel_id=1, source_target_pairs={{1,0},{2,1},{3,2},{4,3},{5,4},{6,5},{7,6},{8,7},{9,8},{10,9},{11,1... | collective-permute-start | bytes 442376 | tf_op jit(solution)/shard_map/ppermute | solution.py:23
  4.4 167.7 %collective-permute-start.1 = (f32[48,2,1,384]{3,0,2,1:T(8,128)S(1)}, f32[48,2,1,384]{3,0,2,1:T(8,128)S(1)}, u32[]{:S(2)}, u32[]{:S(2)}) collective-permute-start(f32[48,2,1,384]{3,0,2,1:T(8,128)S(1)} %get-tuple-element.228), channel_id=1, source_target_pairs={{0,1},{1,2},{2,3},{3,4},{4,5},{5,6},{6,7},{7,8},{8,9},{9,10},{10,1... | collective-permute-start | bytes 442376 | tf_op jit(solution)/shard_map/ppermute | solution.py:21
  8.8 163.4 %collective-permute-start.2 = (f32[48,2,1,384]{3,0,2,1:T(8,128)S(1)}, f32[48,2,1,384]{3,0,2,1:T(8,128)S(1)}, u32[]{:S(2)}, u32[]{:S(2)}) collective-permute-start(f32[48,2,1,384]{3,0,2,1:T(8,128)S(1)} %get-tuple-element.225), channel_id=1, source_target_pairs={{1,0},{2,1},{3,2},{4,3},{5,4},{6,5},{7,6},{8,7},{9,8},{10,9},{11,1... | collective-permute-start | bytes 442376 | tf_op jit(solution)/shard_map/ppermute | solution.py:23
  13.2 158.9 %collective-permute-start.3 = (f32[48,2,1,384]{3,0,2,1:T(8,128)S(1)}, f32[48,2,1,384]{3,0,2,1:T(8,128)S(1)}, u32[]{:S(2)}, u32[]{:S(2)}) collective-permute-start(f32[48,2,1,384]{3,0,2,1:T(8,128)S(1)} %get-tuple-element.224), channel_id=1, source_target_pairs={{0,1},{1,2},{2,3},{3,4},{4,5},{5,6},{6,7},{7,8},{8,9},{9,10},{10,1... | collective-permute-start | bytes 442376 | tf_op jit(solution)/shard_map/ppermute | solution.py:21
  172.1 1.0 copy-start.1
  179.4 18.4 %collective-permute-start.6 = (f32[48,2,1,384]{3,0,2,1:T(8,128)}, f32[48,2,1,384]{3,0,2,1:T(8,128)S(1)}, u32[]{:S(2)}, u32[]{:S(2)}) collective-permute-start(f32[48,2,1,384]{3,0,2,1:T(8,128)} %get-tuple-element.223), channel_id=1, source_target_pairs={{1,0},{2,1},{3,2},{4,3},{5,4},{6,5},{7,6},{8,7},{9,8},{10,9},{11,1... | collective-permute-start | bytes 442376 | tf_op jit(solution)/shard_map/ppermute | solution.py:23
  186.6 11.2 %collective-permute-start.7 = (f32[48,2,1,384]{3,0,2,1:T(8,128)}, f32[48,2,1,384]{3,0,2,1:T(8,128)S(1)}, u32[]{:S(2)}, u32[]{:S(2)}) collective-permute-start(f32[48,2,1,384]{3,0,2,1:T(8,128)} %get-tuple-element.222), channel_id=1, source_target_pairs={{0,1},{1,2},{2,3},{3,4},{4,5},{5,6},{6,7},{7,8},{8,9},{9,10},{10,1... | collective-permute-start | bytes 442376 | tf_op jit(solution)/shard_map/ppermute | solution.py:21
  188.5 9.2 %collective-permute-start.4 = (f32[48,2,1,384]{3,0,2,1:T(8,128)S(1)}, f32[48,2,1,384]{3,0,2,1:T(8,128)S(1)}, u32[]{:S(2)}, u32[]{:S(2)}) collective-permute-start(f32[48,2,1,384]{3,0,2,1:T(8,128)S(1)} %get-tuple-element.227), channel_id=1, source_target_pairs={{1,0},{2,1},{3,2},{4,3},{5,4},{6,5},{7,6},{8,7},{9,8},{10,9},{11,1... | collective-permute-start | bytes 442376 | tf_op jit(solution)/shard_map/ppermute | solution.py:23
  195.8 8.1 %collective-permute-start.5 = (f32[48,2,1,384]{3,0,2,1:T(8,128)S(1)}, f32[48,2,1,384]{3,0,2,1:T(8,128)S(1)}, u32[]{:S(2)}, u32[]{:S(2)}) collective-permute-start(f32[48,2,1,384]{3,0,2,1:T(8,128)S(1)} %get-tuple-element.226), channel_id=1, source_target_pairs={{0,1},{1,2},{2,3},{3,4},{4,5},{5,6},{6,7},{7,8},{8,9},{9,10},{10,1... | collective-permute-start | bytes 442376 | tf_op jit(solution)/shard_map/ppermute | solution.py:21
  203.9 1.5 copy-start.2
  211.3 17.6 %collective-permute-start.10 = (f32[48,2,1,384]{3,0,2,1:T(8,128)}, f32[48,2,1,384]{3,0,2,1:T(8,128)S(1)}, u32[]{:S(2)}, u32[]{:S(2)}) collective-permute-start(f32[48,2,1,384]{3,0,2,1:T(8,128)} %get-tuple-element.221), channel_id=1, source_target_pairs={{1,0},{2,1},{3,2},{4,3},{5,4},{6,5},{7,6},{8,7},{9,8},{10,9},{11,1... | collective-permute-start | bytes 442376 | tf_op jit(solution)/shard_map/ppermute | solution.py:23
  220.5 8.4 %collective-permute-start.11 = (f32[48,2,1,384]{3,0,2,1:T(8,128)}, f32[48,2,1,384]{3,0,2,1:T(8,128)S(1)}, u32[]{:S(2)}, u32[]{:S(2)}) collective-permute-start(f32[48,2,1,384]{3,0,2,1:T(8,128)} %get-tuple-element.220), channel_id=1, source_target_pairs={{0,1},{1,2},{2,3},{3,4},{4,5},{5,6},{6,7},{7,8},{8,9},{9,10},{10,1... | collective-permute-start | bytes 442376 | tf_op jit(solution)/shard_map/ppermute | solution.py:21
  222.5 6.8 %collective-permute-start.8 = (f32[48,2,1,384]{3,0,2,1:T(8,128)S(1)}, f32[48,2,1,384]{3,0,2,1:T(8,128)S(1)}, u32[]{:S(2)}, u32[]{:S(2)}) collective-permute-start(f32[48,2,1,384]{3,0,2,1:T(8,128)S(1)} %get-tuple-element.218), channel_id=1, source_target_pairs={{1,0},{2,1},{3,2},{4,3},{5,4},{6,5},{7,6},{8,7},{9,8},{10,9},{11,1... | collective-permute-start | bytes 442376 | tf_op jit(solution)/shard_map/ppermute | solution.py:23
  224.9 7.6 %collective-permute-start.9 = (f32[48,2,1,384]{3,0,2,1:T(8,128)S(1)}, f32[48,2,1,384]{3,0,2,1:T(8,128)S(1)}, u32[]{:S(2)}, u32[]{:S(2)}) collective-permute-start(f32[48,2,1,384]{3,0,2,1:T(8,128)S(1)} %get-tuple-element.219), channel_id=1, source_target_pairs={{0,1},{1,2},{2,3},{3,4},{4,5},{5,6},{6,7},{7,8},{8,9},{9,10},{10,1... | collective-permute-start | bytes 442376 | tf_op jit(solution)/shard_map/ppermute | solution.py:21
  236.1 17.4 %copy-start = (f32[48,4,384]{2,0,1:T(8,128)S(1)}, f32[48,4,384]{2,0,1:T(8,128)}, u32[]{:S(2)}) copy-start(f32[48,4,384]{2,0,1:T(8,128)} %get-tuple-element.216) | copy-start | bytes 884740
  237.3 11.2 %collective-permute-start.12 = (f32[48,4,1,384]{3,0,2,1:T(8,128)S(1)}, f32[48,4,1,384]{3,0,2,1:T(8,128)S(1)}, u32[]{:S(2)}, u32[]{:S(2)}) collective-permute-start(f32[48,4,1,384]{3,0,2,1:T(8,128)S(1)} %get-tuple-element.204), channel_id=1, source_target_pairs={{1,0},{2,1},{3,2},{4,3},{5,4},{6,5},{7,6},{8,7},{9,8},{10,9},{11,1... | collective-permute-start | bytes 884744 | tf_op jit(solution)/shard_map/ppermute | solution.py:23
  246.5 5.6 collective-permute-start.13
  254.2 9.9 %collective-permute-start.14 = (f32[48,4,1,384]{3,0,2,1:T(8,128)S(1)}, f32[48,4,1,384]{3,0,2,1:T(8,128)S(1)}, u32[]{:S(2)}, u32[]{:S(2)}) collective-permute-start(f32[48,4,1,384]{3,0,2,1:T(8,128)S(1)} %get-tuple-element.202), channel_id=1, source_target_pairs={{1,0},{2,1},{3,2},{4,3},{5,4},{6,5},{7,6},{8,7},{9,8},{10,9},{11,1... | collective-permute-start | bytes 884744 | tf_op jit(solution)/shard_map/ppermute | solution.py:23
  262.2 5.6 collective-permute-start.15
  269.9 12.6 %collective-permute-start.16 = (f32[48,4,1,384]{3,0,2,1:T(8,128)S(1)}, f32[48,4,1,384]{3,0,2,1:T(8,128)S(1)}, u32[]{:S(2)}, u32[]{:S(2)}) collective-permute-start(f32[48,4,1,384]{3,0,2,1:T(8,128)S(1)} %get-tuple-element.200), channel_id=1, source_target_pairs={{1,0},{2,1},{3,2},{4,3},{5,4},{6,5},{7,6},{8,7},{9,8},{10,9},{11,1... | collective-permute-start | bytes 884744 | tf_op jit(solution)/shard_map/ppermute | solution.py:23
  280.6 5.6 collective-permute-start.17
  292.6 215.9 %all-to-all-start = ((f32[16,1,48,2,4,384]{5,4,3,2,1,0:T(4,128)}), f32[16,1,48,2,4,384]{5,4,3,2,1,0:T(4,128)}, u32[]{:S(2)}, u32[]{:S(2)}) async-start(f32[16,1,48,2,4,384]{5,4,3,2,1,0:T(4,128)} %stack.3), calls=%async_computation | async-start | bytes 18874368 | tf_op jit(solution)/shard_map/all_to_all | solution.py:139
